TPU v7x, 32 devices: a whole 2x2x4 slice. The times are simulated.
32 devices in a mesh: row: 4 (over y, core), col: 8 (over z, x).
Axes of the slice: x: 2, y: 2, z: 4, core: 2. Of those that a mesh axis runs over, the one named last changes fastest.
Arguments:
- transition: bfloat16 [32768, 32768], P('row', 'col'), may hold values from 1.5258789e-06 to 0.0024414062, as said below
- emission: bfloat16 [96, 32768], P(None, 'col'), may hold values from 0.0099487305 to 1
- token_ids: int32 [2, 192], replicated, may hold values from 0 to 95
- forward: bfloat16 [2, 192, 32768], P(None, 'col', 'row'), may hold values from 3.0517578e-06 to 0.0008239746, as said below
- backward_last: float32 [192, 32768], P('row', 'col'), may hold values from 0.1 to 10
Outputs:
- backward: float32 [2, 192, 32768], P(None, 'col', 'row')
- counts: float32 [32768, 1024], P('row', 'col')
Inputs may be any that keep to these rules, and one draw needn't show every extreme that they name: Positive transition weights. Positive forward weights.
All inputs are finite; a program needn't handle non-finite values.
Results may differ from a plain program's by a relative error of at most 0.00048.
Values may be sent and summed in bfloat16 or wider, within the bound.
A program may use at most 192 MiB of HBM per device.

v0:
```python
import jax
import jax.numpy as jnp
from jax import lax
from jax.sharding import PartitionSpec as P

H = 32768
N = 192
DW = 128
CHUNKS = 2


def reduce_scatter(partial, scale, col_count, col_index, local_seqs):
    half = col_count // 2
    width = partial.shape[1]
    scaled = (partial * scale).reshape(half, 2, local_seqs, width)
    side = col_index % 2
    away = lax.dynamic_index_in_dim(scaled, 1 - side, 1, keepdims=False).astype(jnp.float16)
    got = lax.ppermute(away, "col", [(c, c ^ 1) for c in range(col_count)])
    pair = lax.dynamic_index_in_dim(scaled, side, 1, keepdims=False) + got.astype(jnp.float32)
    here = col_index // 2
    total = lax.dynamic_index_in_dim(pair, here, 0, keepdims=False)
    packed = pair.astype(jnp.float16)
    for k in range(1, half):
        piece = lax.dynamic_index_in_dim(packed, (here + k) % half, 0, keepdims=False)
        got = lax.ppermute(piece, "col", [(c, (c + 2 * k) % col_count) for c in range(col_count)])
        total = total + got.astype(jnp.float32)
    return total


def on_device(transition, emission, token_ids, forward, backward_last):
    row_count = lax.axis_size("row")
    col_count = lax.axis_size("col")
    row_index = lax.axis_index("row")
    col_index = lax.axis_index("col")
    ratio = col_count // row_count
    local_seqs = forward.shape[1]
    row_seqs = backward_last.shape[0]
    block_src = transition.shape[0]
    block_dst = transition.shape[1]
    seq_total = local_seqs * col_count
    forward_all = [None, lax.all_gather(forward[1], "col", axis=0, tiled=True)]
    columns = lax.broadcasted_iota(jnp.int32, (row_seqs, emission.shape[0]), 1)
    window = transition[:, :DW]
    totals = jnp.zeros((block_src, DW), jnp.float32)
    outputs = [None, None]
    beta = backward_last
    scale = jnp.full((seq_total, 1), 64.0, jnp.float32)
    chunk = block_src // CHUNKS
    for step in (1, 0):
        tokens = lax.dynamic_slice_in_dim(token_ids[step], row_index * row_seqs, row_seqs, 0)
        onehot = (tokens[:, None] == columns).astype(jnp.bfloat16)
        emitted = jnp.dot(onehot, emission, preferred_element_type=jnp.float32)
        local_back = (emitted * beta).astype(jnp.bfloat16)
        weighted_back = lax.all_gather(local_back, "row", axis=0, tiled=True)
        pieces = []
        norm = jnp.zeros((seq_total,), jnp.float32)
        mass = jnp.zeros((seq_total,), jnp.float32)
        if step == 0:
            forward_all[0] = lax.all_gather(forward[0], "col", axis=0, tiled=True)
        for k in range(CHUNKS):
            rows = slice(k * chunk, (k + 1) * chunk)
            partial = lax.dot_general(
                weighted_back,
                transition[rows],
                (((1,), (1,)), ((), ())),
                preferred_element_type=jnp.float32,
            )
            norm = norm + jnp.sum(forward_all[step][:, rows].astype(jnp.float32) * partial, axis=1)
            mass = mass + jnp.sum(partial, axis=1)
            pieces.append(reduce_scatter(partial, scale, col_count, col_index, local_seqs))
        if step == 1:
            both = lax.psum(jnp.stack([norm, mass]), ("row", "col"))
            normal_all = both[0]
        else:
            normal_all = lax.psum(norm, ("row", "col"))
        normal_mine = lax.dynamic_slice_in_dim(normal_all, col_index * local_seqs, local_seqs, 0)
        scale_mine = lax.dynamic_slice_in_dim(scale, col_index * local_seqs, local_seqs, 0)
        mine = jnp.concatenate(pieces, axis=1) / (scale_mine * normal_mine[:, None])
        outputs[step] = mine
        if step == 1:
            halves = mine.reshape(local_seqs, ratio, block_dst)
            arrived = []
            for p in range(ratio):
                part = lax.dynamic_index_in_dim(halves, (col_index + p) % ratio, 1, keepdims=False)
                moves = []
                for r in range(row_count):
                    for c in range(col_count):
                        h = (c + p) % ratio
                        moves.append((r * col_count + c, c // ratio * col_count + r * ratio + h))
                arrived.append(lax.ppermute(part, ("row", "col"), moves))
            turned = jnp.stack([arrived[-i % ratio] for i in range(ratio)] * 2)
            start = (ratio - col_index % ratio) % ratio
            beta = lax.dynamic_slice_in_dim(turned, start, ratio, 0).reshape(row_seqs, block_dst)
            scale = (16777216.0 * both[0] / both[1])[:, None]
        scaled = (forward_all[step].astype(jnp.float32) / normal_all[:, None]).astype(jnp.bfloat16)
        totals = totals + lax.dot_general(
            scaled,
            weighted_back[:, :DW],
            (((0,), (0,)), ((), ())),
            preferred_element_type=jnp.float32,
        )
    counts = window.astype(jnp.float32) * totals * (H * H / N)
    return (jnp.stack(outputs), counts)


def solution(mesh):
    in_specs = (P("row", "col"), P(None, "col"), P(), P(None, "col", "row"), P("row", "col"))
    out_specs = (P(None, "col", "row"), P("row", "col"))
    return jax.shard_map(
        on_device, mesh=mesh, in_specs=in_specs, out_specs=out_specs, check_vma=False
    )
```

profile of v0, /device:TPU:0, one launch (start us, length us, event | category | flops | bytes accessed | tf_op | source)
XLA Modules:
  0.0 469.5 jit_solution(5049262565942433598)
XLA Ops:
  7.2 0.8 fusion.52
  8.1 0.3 copy-done
  8.3 2.2 fusion.10
  10.6 2.0 fusion.50
  12.8 20.2 %all-gather.7.cloned.1.call-done = bf16[192,4096]{1,0:T(8,128)(2,1)} async-done(((bf16[48,4096]{1,0:T(8,128)(2,1)}), bf16[192,4096]{1,0:T(8,128)(2,1)}) %all-gather.7.cloned.1.call-update) | async-done | bytes 1572880 | tf_op jit(solution)/shard_map/all_gather | solution.py:54
  33.1 21.2 %fusion.6 = f32[192,4096]{1,0:T(8,128)} fusion(bf16[192,4096]{1,0:T(8,128)(2,1)} %all-gather.7.cloned.1.call-done, bf16[8192,4096]{1,0:T(8,128)(2,1)} %param.5), kind=kOutput, calls=%fused_computation.6 | convolution fusion | flops 6442450944 | bytes 38273024 | tf_op jit(solution)/shard_map/dot_general | solution.py:62
  54.3 42.0 %all-gather.11.cloned.1.call-done = bf16[1,192,8192]{2,1,0:T(8,128)(2,1)} async-done(((bf16[1,24,8192]{2,1,0:T(8,128)(2,1)}), bf16[1,192,8192]{2,1,0:T(8,128)(2,1)}) %all-gather.11.cloned.1.call-update) | async-done | bytes 3145744 | tf_op jit(solution)/shard_map/all_gather | solution.py:41
  96.3 20.1 %multiply_reduce_fusion.2 = (f32[192]{0:T(256)S(1)}, f32[192]{0:T(256)S(1)}, f32[192]{0:T(256)S(1)}, f32[192]{0:T(256)S(1)}, f32[192,4096]{1,0:T(8,128)}, /*index=5*/f32[192,4096]{1,0:T(8,128)}) fusion(bf16[192,8192]{1,0:T(8,128)(2,1)} %bitcast.147, f32[192,4096]{1,0:T(8,128)} %fusion.6, bf16[192,4096]{1,0:T(8,128)(2,1)S(1)} %copy-done.6, ...), kind=kOutput, calls=%fused_computation.18 | convolution fusion | flops 6450315264 | bytes 47713280 | tf_op jit(solution)/shard_map/dot_general | solution.py:62
  116.4 2.4 fusion.14
  118.8 0.6 collective-permute-start.4
  119.4 1.5 fusion.13
  120.9 1.5 collective-permute-start
  122.4 65.4 %psum.14 = f32[2,192]{1,0:T(2,128)S(1)} all-reduce(f32[2,192]{1,0:T(2,128)S(1)} %pad_maximum_fusion.1), channel_id=1, replica_groups=mesh['row'=4,'col'=8] {'row','col'}, use_global_device_ids=true, to_apply=%region_4.5 | all-reduce | flops 384 | bytes 3072 | tf_op jit(solution)/shard_map/psum | solution.py:72
  188.0 1.8 fusion.49
  189.9 0.9 collective-permute-start.5
  190.8 2.9 collective-permute-start.7
  193.8 0.3 fusion.48
  194.2 0.6 collective-permute-start.1
  194.8 3.3 collective-permute-start.3
  198.0 1.5 collective-permute-done.5
  199.6 6.6 %collective-permute-start.2 = (f16[24,4096]{1,0:T(8,128)(2,1)S(1)}, f16[24,4096]{1,0:T(8,128)(2,1)S(1)}, u32[]{:S(2)}, u32[]{:S(2)}) collective-permute-start(f16[24,4096]{1,0:T(8,128)(2,1)S(1)} %get-tuple-element.36), channel_id=1, source_target_pairs={{0,4},{1,5},{2,6},{3,7},{4,0},{5,1},{6,2},{7,3},{8,12},{9,13},{10,... | collective-permute-start | bytes 589832 | tf_op jit(solution)/shard_map/ppermute | solution.py:25
  206.2 12.6 %collective-permute-done.6 = f16[24,4096]{1,0:T(8,128)(2,1)S(1)} collective-permute-done((f16[24,4096]{1,0:T(8,128)(2,1)S(1)}, f16[24,4096]{1,0:T(8,128)(2,1)S(1)}, u32[]{:S(2)}, u32[]{:S(2)}) %collective-permute-start.6) | collective-permute-done | bytes 196640 | tf_op jit(solution)/shard_map/ppermute | solution.py:25
  218.9 7.1 %collective-permute-done.2 = f16[24,4096]{1,0:T(8,128)(2,1)S(1)} collective-permute-done((f16[24,4096]{1,0:T(8,128)(2,1)S(1)}, f16[24,4096]{1,0:T(8,128)(2,1)S(1)}, u32[]{:S(2)}, u32[]{:S(2)}) %collective-permute-start.2) | collective-permute-done | bytes 196640 | tf_op jit(solution)/shard_map/ppermute | solution.py:25
  226.2 1.4 collective-permute-start.9
  227.7 0.7 collective-permute-start.8
  228.5 13.4 %collective-permute-done.9 = f32[24,4096]{1,0:T(8,128)S(1)} collective-permute-done((f32[24,4096]{1,0:T(8,128)S(1)}, f32[24,4096]{1,0:T(8,128)S(1)}, u32[]{:S(2)}, u32[]{:S(2)}) %collective-permute-start.9) | collective-permute-done | bytes 393248 | tf_op jit(solution)/shard_map/ppermute | solution.py:90
  242.0 1.1 fusion.20
  243.4 0.3 all-gather.13.cloned.1.call-update
  243.7 5.4 %fusion.12 = f32[8192,128]{1,0:T(8,128)} fusion(f32[192]{0:T(256)S(1)} %bitcast.143, bf16[192,4096]{1,0:T(8,128)(2,1)} %all-gather.7.cloned.1.call-done, bf16[1,192,8192]{2,1,0:T(8,128)(2,1)} %all-gather.11.cloned.1.call-done), kind=kOutput, calls=%fused_computation.20 | convolution fusion | flops 407371776 | bytes 7389952 | tf_op jit(solution)/shard_map/dot_general | solution.py:96
  249.3 32.2 %all-gather.9.cloned.1.call-done = bf16[192,4096]{1,0:T(8,128)(2,1)} async-done(((bf16[48,4096]{1,0:T(8,128)(2,1)}), bf16[192,4096]{1,0:T(8,128)(2,1)}) %all-gather.9.cloned.1.call-update) | async-done | bytes 1572880 | tf_op jit(solution)/shard_map/all_gather | solution.py:54
  281.4 21.3 %fusion.4 = f32[192,4096]{1,0:T(8,128)} fusion(bf16[192,4096]{1,0:T(8,128)(2,1)} %all-gather.9.cloned.1.call-done, bf16[8192,4096]{1,0:T(8,128)(2,1)} %param.5), kind=kOutput, calls=%fused_computation.4 | convolution fusion | flops 6442450944 | bytes 38273024 | tf_op jit(solution)/shard_map/dot_general | solution.py:62
  302.8 41.2 %all-gather.13.cloned.1.call-done = bf16[1,192,8192]{2,1,0:T(8,128)(2,1)} async-done(((bf16[1,24,8192]{2,1,0:T(8,128)(2,1)}), bf16[1,192,8192]{2,1,0:T(8,128)(2,1)}) %all-gather.13.cloned.1.call-update) | async-done | bytes 3145744 | tf_op jit(solution)/shard_map/all_gather | solution.py:59
  344.0 20.1 %multiply_reduce_fusion = (f32[192]{0:T(256)S(1)}, f32[192]{0:T(256)S(1)}, f32[192,4096]{1,0:T(8,128)}, f32[192,4096]{1,0:T(8,128)}) fusion(bf16[192,8192]{1,0:T(8,128)(2,1)} %bitcast.148, f32[192,4096]{1,0:T(8,128)} %fusion.4, f32[192]{0:T(256)S(1)} %multiply_divide_fusion, bf16[192,4096]{1,0:T(8,128)(2,1)S(1)} %copy-done.7, bf16[8192,4096]{1,0:T(8,128)(2,1)} %param.5), kind=kOutput, calls=%fused_computation.16 | convolution fusion | flops 6448742400 | bytes 47712512 | tf_op jit(solution)/shard_map/dot_general | solution.py:62
  364.1 39.2 %psum.15 = f32[192]{0:T(256)S(1)} all-reduce(f32[192]{0:T(256)S(1)} %add.236), channel_id=1, replica_groups=mesh['row'=4,'col'=8] {'row','col'}, use_global_device_ids=true, to_apply=%region_7.8 | all-reduce | flops 192 | bytes 1536 | tf_op jit(solution)/shard_map/psum | solution.py:75
  403.3 1.6 fusion.15
  405.0 1.5 fusion.16
  406.5 2.3 collective-permute-start.14
  408.9 6.6 %fusion.9 = f32[8192,128]{1,0:T(8,128)} fusion(f32[8192,128]{1,0:T(8,128)} %fusion.12, f32[192]{0:T(256)S(1)} %psum.15, bf16[8192,4096]{1,0:T(8,128)(2,1)} %param.5, bf16[192,4096]{1,0:T(8,128)(2,1)S(1)} %copy-done.7, bf16[1,192,8192]{2,1,0:T(8,128)(2,1)S(1)} %copy-done.5), kind=kOutput, calls=%fused_computation.10 | convolution fusion | flops 411566080 | bytes 13681664 | tf_op jit(solution)/shard_map/dot_general | solution.py:96
  415.6 11.8 %collective-permute-done.14 = f16[4,24,4096]{2,1,0:T(8,128)(2,1)S(1)} collective-permute-done((f16[4,24,4096]{2,1,0:T(8,128)(2,1)S(1)}, f16[4,24,4096]{2,1,0:T(8,128)(2,1)S(1)}, u32[]{:S(2)}, u32[]{:S(2)}) %collective-permute-start.14) | collective-permute-done | bytes 786464 | tf_op jit(solution)/shard_map/ppermute | solution.py:18
  427.7 0.7 collective-permute-start.15
  428.3 3.2 collective-permute-start.17
  431.6 10.9 %collective-permute-done.10 = f16[4,24,4096]{2,1,0:T(8,128)(2,1)S(1)} collective-permute-done((f16[4,24,4096]{2,1,0:T(8,128)(2,1)S(1)}, f16[4,24,4096]{2,1,0:T(8,128)(2,1)S(1)}, u32[]{:S(2)}, u32[]{:S(2)}) %collective-permute-start.10) | collective-permute-done | bytes 786464 | tf_op jit(solution)/shard_map/ppermute | solution.py:18
  442.9 0.6 collective-permute-start.11
  443.5 3.3 collective-permute-start.13
  446.9 5.7 %collective-permute-done.11 = f16[24,4096]{1,0:T(8,128)(2,1)S(1)} collective-permute-done((f16[24,4096]{1,0:T(8,128)(2,1)S(1)}, f16[24,4096]{1,0:T(8,128)(2,1)S(1)}, u32[]{:S(2)}, u32[]{:S(2)}) %collective-permute-start.11) | collective-permute-done | bytes 196640 | tf_op jit(solution)/shard_map/ppermute | solution.py:25
  452.6 0.9 collective-permute-done.13
  453.5 8.0 %collective-permute-done.12 = f16[24,4096]{1,0:T(8,128)(2,1)S(1)} collective-permute-done((f16[24,4096]{1,0:T(8,128)(2,1)S(1)}, f16[24,4096]{1,0:T(8,128)(2,1)S(1)}, u32[]{:S(2)}, u32[]{:S(2)}) %collective-permute-start.12) | collective-permute-done | bytes 196640 | tf_op jit(solution)/shard_map/ppermute | solution.py:25
  461.7 1.3 pad_maximum_fusion
  (60 shorter events, 2.8 us)
Async XLA Ops:
  7.2 1.2 copy-start
  7.2 25.9 %all-gather.7.cloned.1.call-start = ((), (), s32[]{:S(2)}) async-start(), calls=%async_computation | async-start | bytes 1966080 | tf_op jit(solution)/shard_map/all_gather | solution.py:54
  10.6 85.7 %all-gather.11.cloned.1.call-start = ((), (), s32[]{:S(2)}) async-start(), calls=%async_computation.2 | async-start | bytes 3538944 | tf_op jit(solution)/shard_map/all_gather | solution.py:41
  12.7 268.8 %all-gather.9.cloned.1.call-start = ((), (), s32[]{:S(2)}) async-start(), calls=%async_computation.1 | async-start | bytes 1966080 | tf_op jit(solution)/shard_map/all_gather | solution.py:54
  33.1 63.2 %copy-start.6 = (bf16[192,4096]{1,0:T(8,128)(2,1)S(1)}, bf16[192,4096]{1,0:T(8,128)(2,1)}, u32[]{:S(2)}) copy-start(bf16[192,4096]{1,0:T(8,128)(2,1)} %all-gather.7.cloned.1.call-done) | copy-start | bytes 4718596
  118.8 69.1 %collective-permute-start.4 = (f16[4,24,4096]{2,1,0:T(8,128)(2,1)}, f16[4,24,4096]{2,1,0:T(8,128)(2,1)S(1)}, u32[]{:S(2)}, u32[]{:S(2)}) collective-permute-start(f16[4,24,4096]{2,1,0:T(8,128)(2,1)} %fusion.14), channel_id=1, source_target_pairs={{0,1},{1,0},{2,3},{3,2},{4,5},{5,4},{6,7},{7,6},{8,9},{9,8},{10,11... | collective-permute-start | bytes 2359304 | tf_op jit(solution)/shard_map/ppermute | solution.py:18
  120.9 72.9 %collective-permute-start = (f16[4,24,4096]{2,1,0:T(8,128)(2,1)S(1)}, f16[4,24,4096]{2,1,0:T(8,128)(2,1)S(1)}, u32[]{:S(2)}, u32[]{:S(2)}) collective-permute-start(f16[4,24,4096]{2,1,0:T(8,128)(2,1)S(1)} %fusion.13), channel_id=1, source_target_pairs={{0,1},{1,0},{2,3},{3,2},{4,5},{5,4},{6,7},{7,6},{8,9},{9,8},{10,11... | collective-permute-start | bytes 2359304 | tf_op jit(solution)/shard_map/ppermute | solution.py:18
  187.9 5.9 %copy-start.2 = (f32[192,4096]{1,0:T(8,128)S(1)}, f32[192,4096]{1,0:T(8,128)}, u32[]{:S(2)}) copy-start(f32[192,4096]{1,0:T(8,128)} %get-tuple-element.18) | copy-start | bytes 9437188
  189.9 9.7 %collective-permute-start.5 = (f16[24,4096]{1,0:T(8,128)(2,1)S(1)}, f16[24,4096]{1,0:T(8,128)(2,1)S(1)}, u32[]{:S(2)}, u32[]{:S(2)}) collective-permute-start(f16[24,4096]{1,0:T(8,128)(2,1)S(1)} %get-tuple-element.37), channel_id=1, source_target_pairs={{0,2},{1,3},{2,4},{3,5},{4,6},{5,7},{6,0},{7,1},{8,10},{9,11},{10,... | collective-permute-start | bytes 589832 | tf_op jit(solution)/shard_map/ppermute | solution.py:25
  190.8 15.3 %collective-permute-start.7 = (f16[24,4096]{1,0:T(8,128)(2,1)S(1)}, f16[24,4096]{1,0:T(8,128)(2,1)S(1)}, u32[]{:S(2)}, u32[]{:S(2)}) collective-permute-start(f16[24,4096]{1,0:T(8,128)(2,1)S(1)} %get-tuple-element.38), channel_id=1, source_target_pairs={{0,6},{1,7},{2,0},{3,1},{4,2},{5,3},{6,4},{7,5},{8,14},{9,15},{10,... | collective-permute-start | bytes 589832 | tf_op jit(solution)/shard_map/ppermute | solution.py:25
  193.8 25.0 %collective-permute-start.6 = (f16[24,4096]{1,0:T(8,128)(2,1)S(1)}, f16[24,4096]{1,0:T(8,128)(2,1)S(1)}, u32[]{:S(2)}, u32[]{:S(2)}) collective-permute-start(f16[24,4096]{1,0:T(8,128)(2,1)S(1)} %get-tuple-element.39), channel_id=1, source_target_pairs={{0,4},{1,5},{2,6},{3,7},{4,0},{5,1},{6,2},{7,3},{8,12},{9,13},{10,... | collective-permute-start | bytes 589832 | tf_op jit(solution)/shard_map/ppermute | solution.py:25
  194.2 24.7 %collective-permute-start.1 = (f16[24,4096]{1,0:T(8,128)(2,1)S(1)}, f16[24,4096]{1,0:T(8,128)(2,1)S(1)}, u32[]{:S(2)}, u32[]{:S(2)}) collective-permute-start(f16[24,4096]{1,0:T(8,128)(2,1)S(1)} %get-tuple-element.34), channel_id=1, source_target_pairs={{0,2},{1,3},{2,4},{3,5},{4,6},{5,7},{6,0},{7,1},{8,10},{9,11},{10,... | collective-permute-start | bytes 589832 | tf_op jit(solution)/shard_map/ppermute | solution.py:25
  194.8 24.1 %collective-permute-start.3 = (f16[24,4096]{1,0:T(8,128)(2,1)S(1)}, f16[24,4096]{1,0:T(8,128)(2,1)S(1)}, u32[]{:S(2)}, u32[]{:S(2)}) collective-permute-start(f16[24,4096]{1,0:T(8,128)(2,1)S(1)} %get-tuple-element.35), channel_id=1, source_target_pairs={{0,6},{1,7},{2,0},{3,1},{4,2},{5,3},{6,4},{7,5},{8,14},{9,15},{10,... | collective-permute-start | bytes 589832 | tf_op jit(solution)/shard_map/ppermute | solution.py:25
  199.6 26.4 %collective-permute-start.2 = (f16[24,4096]{1,0:T(8,128)(2,1)S(1)}, f16[24,4096]{1,0:T(8,128)(2,1)S(1)}, u32[]{:S(2)}, u32[]{:S(2)}) collective-permute-start(f16[24,4096]{1,0:T(8,128)(2,1)S(1)} %get-tuple-element.36), channel_id=1, source_target_pairs={{0,4},{1,5},{2,6},{3,7},{4,0},{5,1},{6,2},{7,3},{8,12},{9,13},{10,... | collective-permute-start | bytes 589832 | tf_op jit(solution)/shard_map/ppermute | solution.py:25
  226.2 15.6 %collective-permute-start.9 = (f32[24,4096]{1,0:T(8,128)S(1)}, f32[24,4096]{1,0:T(8,128)S(1)}, u32[]{:S(2)}, u32[]{:S(2)}) collective-permute-start(f32[24,4096]{1,0:T(8,128)S(1)} %get-tuple-element.32), channel_id=1, source_target_pairs={{0,1},{1,0},{2,9},{3,8},{4,17},{5,16},{6,25},{7,24},{8,3},{9,2},{1... | collective-permute-start | bytes 1179656 | tf_op jit(solution)/shard_map/ppermute | solution.py:90
  227.7 14.2 %collective-permute-start.8 = (f32[24,4096]{1,0:T(8,128)S(1)}, f32[24,4096]{1,0:T(8,128)S(1)}, u32[]{:S(2)}, u32[]{:S(2)}) collective-permute-start(f32[24,4096]{1,0:T(8,128)S(1)} %get-tuple-element.33), channel_id=1, source_target_pairs={{0,0},{1,1},{2,8},{3,9},{4,16},{5,17},{6,24},{7,25},{8,2},{9,3},{1... | collective-permute-start | bytes 1179656 | tf_op jit(solution)/shard_map/ppermute | solution.py:90
  243.1 100.8 %all-gather.13.cloned.1.call-start = ((), (), s32[]{:S(2)}) async-start(), calls=%async_computation.3 | async-start | bytes 3538944 | tf_op jit(solution)/shard_map/all_gather | solution.py:59
  281.4 62.5 %copy-start.7 = (bf16[192,4096]{1,0:T(8,128)(2,1)S(1)}, bf16[192,4096]{1,0:T(8,128)(2,1)}, u32[]{:S(2)}) copy-start(bf16[192,4096]{1,0:T(8,128)(2,1)} %all-gather.9.cloned.1.call-done) | copy-start | bytes 4718596
  403.3 5.7 %copy-start.5 = (bf16[1,192,8192]{2,1,0:T(8,128)(2,1)S(1)}, bf16[1,192,8192]{2,1,0:T(8,128)(2,1)}, u32[]{:S(2)}) copy-start(bf16[1,192,8192]{2,1,0:T(8,128)(2,1)} %all-gather.13.cloned.1.call-done) | copy-start | bytes 9437188
  406.5 20.8 %copy-start.4 = (f32[192,4096]{1,0:T(8,128)S(1)}, f32[192,4096]{1,0:T(8,128)}, u32[]{:S(2)}) copy-start(f32[192,4096]{1,0:T(8,128)} %get-tuple-element.17) | copy-start | bytes 9437188
  406.5 20.8 %collective-permute-start.14 = (f16[4,24,4096]{2,1,0:T(8,128)(2,1)S(1)}, f16[4,24,4096]{2,1,0:T(8,128)(2,1)S(1)}, u32[]{:S(2)}, u32[]{:S(2)}) collective-permute-start(f16[4,24,4096]{2,1,0:T(8,128)(2,1)S(1)} %fusion.16), channel_id=1, source_target_pairs={{0,1},{1,0},{2,3},{3,2},{4,5},{5,4},{6,7},{7,6},{8,9},{9,8},{10,11... | collective-permute-start | bytes 2359304 | tf_op jit(solution)/shard_map/ppermute | solution.py:18
  408.9 33.6 %collective-permute-start.10 = (f16[4,24,4096]{2,1,0:T(8,128)(2,1)S(1)}, f16[4,24,4096]{2,1,0:T(8,128)(2,1)S(1)}, u32[]{:S(2)}, u32[]{:S(2)}) collective-permute-start(f16[4,24,4096]{2,1,0:T(8,128)(2,1)S(1)} %fusion.15), channel_id=1, source_target_pairs={{0,1},{1,0},{2,3},{3,2},{4,5},{5,4},{6,7},{7,6},{8,9},{9,8},{10,11... | collective-permute-start | bytes 2359304 | tf_op jit(solution)/shard_map/ppermute | solution.py:18
  415.6 26.9 %copy-start.3 = (f32[192,4096]{1,0:T(8,128)S(1)}, f32[192,4096]{1,0:T(8,128)}, u32[]{:S(2)}) copy-start(f32[192,4096]{1,0:T(8,128)} %get-tuple-element.16) | copy-start | bytes 9437188
  427.7 19.1 %collective-permute-start.15 = (f16[24,4096]{1,0:T(8,128)(2,1)S(1)}, f16[24,4096]{1,0:T(8,128)(2,1)S(1)}, u32[]{:S(2)}, u32[]{:S(2)}) collective-permute-start(f16[24,4096]{1,0:T(8,128)(2,1)S(1)} %get-tuple-element.29), channel_id=1, source_target_pairs={{0,2},{1,3},{2,4},{3,5},{4,6},{5,7},{6,0},{7,1},{8,10},{9,11},{10,... | collective-permute-start | bytes 589832 | tf_op jit(solution)/shard_map/ppermute | solution.py:25
  428.3 18.4 %collective-permute-start.17 = (f16[24,4096]{1,0:T(8,128)(2,1)S(1)}, f16[24,4096]{1,0:T(8,128)(2,1)S(1)}, u32[]{:S(2)}, u32[]{:S(2)}) collective-permute-start(f16[24,4096]{1,0:T(8,128)(2,1)S(1)} %get-tuple-element.30), channel_id=1, source_target_pairs={{0,6},{1,7},{2,0},{3,1},{4,2},{5,3},{6,4},{7,5},{8,14},{9,15},{10,... | collective-permute-start | bytes 589832 | tf_op jit(solution)/shard_map/ppermute | solution.py:25
  431.6 15.2 %collective-permute-start.16 = (f16[24,4096]{1,0:T(8,128)(2,1)S(1)}, f16[24,4096]{1,0:T(8,128)(2,1)S(1)}, u32[]{:S(2)}, u32[]{:S(2)}) collective-permute-start(f16[24,4096]{1,0:T(8,128)(2,1)S(1)} %get-tuple-element.31), channel_id=1, source_target_pairs={{0,4},{1,5},{2,6},{3,7},{4,0},{5,1},{6,2},{7,3},{8,12},{9,13},{10,... | collective-permute-start | bytes 589832 | tf_op jit(solution)/shard_map/ppermute | solution.py:25
  442.9 9.7 %collective-permute-start.11 = (f16[24,4096]{1,0:T(8,128)(2,1)S(1)}, f16[24,4096]{1,0:T(8,128)(2,1)S(1)}, u32[]{:S(2)}, u32[]{:S(2)}) collective-permute-start(f16[24,4096]{1,0:T(8,128)(2,1)S(1)} %get-tuple-element.26), channel_id=1, source_target_pairs={{0,2},{1,3},{2,4},{3,5},{4,6},{5,7},{6,0},{7,1},{8,10},{9,11},{10,... | collective-permute-start | bytes 589832 | tf_op jit(solution)/shard_map/ppermute | solution.py:25
  443.5 10.0 %collective-permute-start.13 = (f16[24,4096]{1,0:T(8,128)(2,1)S(1)}, f16[24,4096]{1,0:T(8,128)(2,1)S(1)}, u32[]{:S(2)}, u32[]{:S(2)}) collective-permute-start(f16[24,4096]{1,0:T(8,128)(2,1)S(1)} %get-tuple-element.27), channel_id=1, source_target_pairs={{0,6},{1,7},{2,0},{3,1},{4,2},{5,3},{6,4},{7,5},{8,14},{9,15},{10,... | collective-permute-start | bytes 589832 | tf_op jit(solution)/shard_map/ppermute | solution.py:25
  446.8 14.7 %collective-permute-start.12 = (f16[24,4096]{1,0:T(8,128)(2,1)S(1)}, f16[24,4096]{1,0:T(8,128)(2,1)S(1)}, u32[]{:S(2)}, u32[]{:S(2)}) collective-permute-start(f16[24,4096]{1,0:T(8,128)(2,1)S(1)} %get-tuple-element.28), channel_id=1, source_target_pairs={{0,4},{1,5},{2,6},{3,7},{4,0},{5,1},{6,2},{7,3},{8,12},{9,13},{10,... | collective-permute-start | bytes 589832 | tf_op jit(solution)/shard_map/ppermute | solution.py:25
  446.8 16.2 %copy-start.1 = (bf16[96,4096]{1,0:T(8,128)(2,1)S(1)}, bf16[96,4096]{1,0:T(8,128)(2,1)}, u32[]{:S(2)}) copy-start(bf16[96,4096]{1,0:T(8,128)(2,1)} %param.6) | copy-start | bytes 2359300
Sparse Core Ops, SparseCore 0:
  10.7 22.3 all-gather.6
  35.8 60.4 all-gather.10
  243.3 38.1 all-gather.8
  283.5 60.4 all-gather.12
where the time goes:
time: 470 us; the launch traced here: 469 us
  waiting for transfers between devices  208 us (44%)
  blocking collectives  105 us (22%)
  matrix products  98.1 us (21%)
  starting transfers between devices  29 us (6%)
  between operations  14.1 us (3%)
  other arithmetic  11.9 us (3%)
    dot_general x4, matrix products, on_device(): lax.dot_general(weighted_back, transition[rows], (((1,), (1,)), ((), ()))...  82.8 us
    psum x1, blocking collectives, on_device(): both = lax.psum(jnp.stack([norm, mass]), ('row', 'col'))  65.4 us
    all_gather x2, waiting for transfers between devices, on_device(): weighted_back = lax.all_gather(local_back, 'row', axis=0, tiled=True)  52.4 us
    all_gather x1, waiting for transfers between devices, on_device(): forward_all = [None, lax.all_gather(forward[1], 'col', axis=0, tiled=True)]  42 us
    all_gather x1, waiting for transfers between devices, on_device(): forward_all[0] = lax.all_gather(forward[0], 'col', axis=0, tiled=True)  41.2 us
    psum x1, blocking collectives, on_device(): normal_all = lax.psum(norm, ('row', 'col'))  39.2 us
    ppermute x12, waiting for transfers between devices, reduce_scatter(): lax.ppermute(piece, 'col', [(c, (c + 2 * k) % col_count) for c in range(c...  35.8 us
    ppermute x4, waiting for transfers between devices, reduce_scatter(): got = lax.ppermute(away, 'col', [(c, c ^ 1) for c in range(col_count)])  22.7 us
  transfers between devices with their start and end apart: 22, of which 13 were waited for; matrix products, arithmetic and copies ran while one was open for 13% of the time, Pallas kernels for 0%

commit v1 on v0

--- a/solution.py
+++ b/solution.py
@@ -7,6 +7,24 @@
 N = 192
 DW = 128
 CHUNKS = 2
+
+
+def ring_gather(array, axis, dim):
+    ways, here, step = (lax.axis_size(axis), lax.axis_index(axis), array.shape[dim])
+    shape = [n * ways if d == dim else n for d, n in enumerate(array.shape)]
+    full = lax.dynamic_update_slice_in_dim(
+        jnp.zeros(shape, array.dtype), array, here * step, axis=dim
+    )
+    going_up = going_down = array
+    for far in range(1, ways // 2 + 1):
+        going_up = lax.ppermute(going_up, axis, [(d, (d + 1) % ways) for d in range(ways)])
+        full = lax.dynamic_update_slice_in_dim(full, going_up, (here - far) % ways * step, axis=dim)
+        if 2 * far < ways:
+            going_down = lax.ppermute(going_down, axis, [(d, (d - 1) % ways) for d in range(ways)])
+            full = lax.dynamic_update_slice_in_dim(
+                full, going_down, (here + far) % ways * step, axis=dim
+            )
+    return full
 
 
 def reduce_scatter(partial, scale, col_count, col_index, local_seqs):
@@ -38,7 +56,7 @@
     block_src = transition.shape[0]
     block_dst = transition.shape[1]
     seq_total = local_seqs * col_count
-    forward_all = [None, lax.all_gather(forward[1], "col", axis=0, tiled=True)]
+    forward_all = [None, ring_gather(forward[1], "col", 0)]
     columns = lax.broadcasted_iota(jnp.int32, (row_seqs, emission.shape[0]), 1)
     window = transition[:, :DW]
     totals = jnp.zeros((block_src, DW), jnp.float32)

time: 470 us -> 491 us (1.045)
  waiting for transfers between devices: 208 us -> 173 us
  starting transfers between devices: 29 us -> 57.7 us
  blocking collectives: 105 us -> 129 us
  matrix products: 98.1 us -> 89.2 us
  local copies, waits for them, and re-layouts: 3.78 us -> 11.9 us
    all_gather x1 -> x0, waiting for transfers between devices: 42 us -> none  [on_device(): forward_all = [None, lax.all_gather(forward[1], 'col', axis=0, tiled=True)]]
    ppermute x0 -> x7, waiting for transfers between devices: none -> 37.9 us  [the longest x4 37.9 us: ring_gather(): lax.ppermute(going_up, axis, [(d, (d + 1) % ways) for d in range(ways)])]
    psum x1, blocking collectives: 39.2 us -> 66.1 us  [on_device(): normal_all = lax.psum(norm, ('row', 'col'))]
    ppermute x4, waiting for transfers between devices: 22.7 us -> 0.01 us  [reduce_scatter(): got = lax.ppermute(away, 'col', [(c, c ^ 1) for c in range(col_count)])]
    ppermute x0 -> x7, starting transfers between devices: none -> 19.5 us  [the longest x4 10.4 us: ring_gather(): lax.ppermute(going_up, axis, [(d, (d + 1) % ways) for d in range(ways)])]
    ppermute x12, starting transfers between devices: 22.1 us -> 31.7 us  [reduce_scatter(): lax.ppermute(piece, 'col', [(c, (c + 2 * k) % col_count) for c in range(c...]
    ppermute x2, waiting for transfers between devices: 13.4 us -> 6.39 us  [on_device(): arrived.append(lax.ppermute(part, ('row', 'col'), moves))]
    dot_general x4, matrix products: 82.8 us -> 76.3 us  [on_device(): lax.dot_general(weighted_back, transition[rows], (((1,), (1,)), ((), ()))...]
  transfers between devices with their start and end apart: 22 -> 28, of which waited for: 13 -> 12; matrix products, arithmetic and copies ran while one was open for 13% -> 10% of each run, Pallas kernels for 0% -> 0%
where the time goes in v1:
time: 491 us; the launch traced here: 490 us
  waiting for transfers between devices  173 us (35%)
  blocking collectives  129 us (26%)
  matrix products  89.2 us (18%)
  starting transfers between devices  57.7 us (12%)
  other arithmetic  15.2 us (3%)
  between operations  14 us (3%)
  local copies, waits for them, and re-layouts  11.9 us (2%)
    dot_general x4, matrix products, on_device(): lax.dot_general(weighted_back, transition[rows], (((1,), (1,)), ((), ()))...  76.3 us
    psum x1, blocking collectives, on_device(): normal_all = lax.psum(norm, ('row', 'col'))  66.1 us
    psum x1, blocking collectives, on_device(): both = lax.psum(jnp.stack([norm, mass]), ('row', 'col'))  62.6 us
    all_gather x2, waiting for transfers between devices, on_device(): weighted_back = lax.all_gather(local_back, 'row', axis=0, tiled=True)  46.5 us
    all_gather x1, waiting for transfers between devices, on_device(): forward_all[0] = lax.all_gather(forward[0], 'col', axis=0, tiled=True)  44.2 us
    ppermute x4, waiting for transfers between devices, ring_gather(): lax.ppermute(going_up, axis, [(d, (d + 1) % ways) for d in range(ways)])  37.9 us
    ppermute x12, waiting for transfers between devices, reduce_scatter(): lax.ppermute(piece, 'col', [(c, (c + 2 * k) % col_count) for c in range(c...  37.7 us
    ppermute x12, starting transfers between devices, reduce_scatter(): lax.ppermute(piece, 'col', [(c, (c + 2 * k) % col_count) for c in range(c...  31.7 us
  transfers between devices with their start and end apart: 28, of which 12 were waited for; matrix products, arithmetic and copies ran while one was open for 10% of the time, Pallas kernels for 0%

profile of v1, /device:TPU:0, one launch (start us, length us, event | category | flops | bytes accessed | tf_op | source)
XLA Modules:
  0.0 490.0 jit_solution(12077105299841465130)
XLA Ops:
  7.2 2.0 fusion.49
  9.3 2.9 collective-permute-start.8
  12.2 3.0 collective-permute-start.9
  16.1 2.2 fusion.10
  18.3 2.1 broadcast_in_dim.2
  21.2 7.8 %collective-permute-done.8 = bf16[24,8192]{1,0:T(8,128)(2,1)S(1)} collective-permute-done((bf16[24,8192]{1,0:T(8,128)(2,1)S(1)}, bf16[24,8192]{1,0:T(8,128)(2,1)S(1)}, u32[]{:S(2)}, u32[]{:S(2)}) %collective-permute-start.8) | collective-permute-done | bytes 393248 | tf_op jit(solution)/shard_map/ppermute | solution.py:20
  29.0 2.5 collective-permute-start.10
  31.5 3.0 collective-permute-start.11
  36.1 11.4 %collective-permute-done.10 = bf16[24,8192]{1,0:T(8,128)(2,1)S(1)} collective-permute-done((bf16[24,8192]{1,0:T(8,128)(2,1)S(1)}, bf16[24,8192]{1,0:T(8,128)(2,1)S(1)}, u32[]{:S(2)}, u32[]{:S(2)}) %collective-permute-start.10) | collective-permute-done | bytes 393248 | tf_op jit(solution)/shard_map/ppermute | solution.py:20
  47.5 2.5 collective-permute-start.12
  50.0 3.0 collective-permute-start.13
  54.6 10.5 %collective-permute-done.12 = bf16[24,8192]{1,0:T(8,128)(2,1)S(1)} collective-permute-done((bf16[24,8192]{1,0:T(8,128)(2,1)S(1)}, bf16[24,8192]{1,0:T(8,128)(2,1)S(1)}, u32[]{:S(2)}, u32[]{:S(2)}) %collective-permute-start.12) | collective-permute-done | bytes 393248 | tf_op jit(solution)/shard_map/ppermute | solution.py:20
  65.1 2.5 collective-permute-start.14
  69.2 8.1 %collective-permute-done.14 = bf16[24,8192]{1,0:T(8,128)(2,1)S(1)} collective-permute-done((bf16[24,8192]{1,0:T(8,128)(2,1)S(1)}, bf16[24,8192]{1,0:T(8,128)(2,1)S(1)}, u32[]{:S(2)}, u32[]{:S(2)}) %collective-permute-start.14) | collective-permute-done | bytes 393248 | tf_op jit(solution)/shard_map/ppermute | solution.py:20
  78.2 18.3 %fusion.6 = f32[192,4096]{1,0:T(8,128)} fusion(bf16[192,4096]{1,0:T(8,128)(2,1)} %all-gather.5.cloned.1.call-done, bf16[8192,4096]{1,0:T(8,128)(2,1)} %param.5), kind=kOutput, calls=%fused_computation.6 | convolution fusion | flops 6442450944 | bytes 38273024 | tf_op jit(solution)/shard_map/dot_general | solution.py:80
  96.5 20.1 %multiply_reduce_fusion.2 = (f32[192]{0:T(256)S(1)}, f32[192]{0:T(256)S(1)}, f32[192]{0:T(256)S(1)}, f32[192]{0:T(256)S(1)}, f32[192,4096]{1,0:T(8,128)}, /*index=5*/f32[192,4096]{1,0:T(8,128)}) fusion(bf16[192,8192]{1,0:T(8,128)(2,1)} %constant_dynamic-update-slice_fusion, f32[192,4096]{1,0:T(8,128)} %fusion.6, bf16[192,4096]{1,0:T(8,128)(2,1)S(1)} %copy-done.6, ...), kind=kOutput, calls=%fused_computation.18 | convolution fusion | flops 6450315264 | bytes 47713280 | tf_op jit(solution)/shard_map/dot_general | solution.py:80
  116.6 2.4 fusion.14
  119.0 1.5 fusion.13
  120.5 2.1 collective-permute-start
  122.6 62.6 %psum.14 = f32[2,192]{1,0:T(2,128)S(1)} all-reduce(f32[2,192]{1,0:T(2,128)S(1)} %pad_maximum_fusion.1), channel_id=1, replica_groups=mesh['row'=4,'col'=8] {'row','col'}, use_global_device_ids=true, to_apply=%region_4.5 | all-reduce | flops 384 | bytes 3072 | tf_op jit(solution)/shard_map/psum | solution.py:90
  185.2 1.8 fusion.48
  187.2 1.9 collective-permute-start.7
  190.8 3.2 collective-permute-start.3
  195.1 9.3 %collective-permute-start.1 = (f16[24,4096]{1,0:T(8,128)(2,1)S(1)}, f16[24,4096]{1,0:T(8,128)(2,1)S(1)}, u32[]{:S(2)}, u32[]{:S(2)}) collective-permute-start(f16[24,4096]{1,0:T(8,128)(2,1)S(1)} %get-tuple-element.34), channel_id=1, source_target_pairs={{0,2},{1,3},{2,4},{3,5},{4,6},{5,7},{6,0},{7,1},{8,10},{9,11},{10,... | collective-permute-start | bytes 589832 | tf_op jit(solution)/shard_map/ppermute | solution.py:43
  204.4 12.2 %collective-permute-done.6 = f16[24,4096]{1,0:T(8,128)(2,1)S(1)} collective-permute-done((f16[24,4096]{1,0:T(8,128)(2,1)S(1)}, f16[24,4096]{1,0:T(8,128)(2,1)S(1)}, u32[]{:S(2)}, u32[]{:S(2)}) %collective-permute-start.6) | collective-permute-done | bytes 196640 | tf_op jit(solution)/shard_map/ppermute | solution.py:43
  216.7 6.3 %collective-permute-done.2 = f16[24,4096]{1,0:T(8,128)(2,1)S(1)} collective-permute-done((f16[24,4096]{1,0:T(8,128)(2,1)S(1)}, f16[24,4096]{1,0:T(8,128)(2,1)S(1)}, u32[]{:S(2)}, u32[]{:S(2)}) %collective-permute-start.2) | collective-permute-done | bytes 196640 | tf_op jit(solution)/shard_map/ppermute | solution.py:43
  224.0 1.4 collective-permute-start.16
  225.5 6.4 %collective-permute-done.16 = f32[24,4096]{1,0:T(8,128)S(1)} collective-permute-done((f32[24,4096]{1,0:T(8,128)S(1)}, f32[24,4096]{1,0:T(8,128)S(1)}, u32[]{:S(2)}, u32[]{:S(2)}) %collective-permute-start.16) | collective-permute-done | bytes 393248 | tf_op jit(solution)/shard_map/ppermute | solution.py:108
  232.0 1.1 fusion.20
  233.9 1.0 maximum_divide_fusion.2
  234.9 46.5 %all-gather.7.cloned.1.call-done = bf16[192,4096]{1,0:T(8,128)(2,1)} async-done(((bf16[48,4096]{1,0:T(8,128)(2,1)}), bf16[192,4096]{1,0:T(8,128)(2,1)}) %all-gather.7.cloned.1.call-update) | async-done | bytes 1572880 | tf_op jit(solution)/shard_map/all_gather | solution.py:72
  281.4 18.5 %fusion.4 = f32[192,4096]{1,0:T(8,128)} fusion(bf16[192,4096]{1,0:T(8,128)(2,1)} %all-gather.7.cloned.1.call-done, bf16[8192,4096]{1,0:T(8,128)(2,1)} %param.5), kind=kOutput, calls=%fused_computation.4 | convolution fusion | flops 6442450944 | bytes 38273024 | tf_op jit(solution)/shard_map/dot_general | solution.py:80
  299.9 44.2 %all-gather.9.cloned.1.call-done = bf16[1,192,8192]{2,1,0:T(8,128)(2,1)} async-done(((bf16[1,24,8192]{2,1,0:T(8,128)(2,1)}), bf16[1,192,8192]{2,1,0:T(8,128)(2,1)}) %all-gather.9.cloned.1.call-update) | async-done | bytes 3145744 | tf_op jit(solution)/shard_map/all_gather | solution.py:77
  344.1 19.4 %multiply_reduce_fusion = (f32[192]{0:T(256)S(1)}, f32[192]{0:T(256)S(1)}, f32[192,4096]{1,0:T(8,128)S(1)}, f32[192,4096]{1,0:T(8,128)}) fusion(bf16[192,8192]{1,0:T(8,128)(2,1)} %bitcast.146, f32[192,4096]{1,0:T(8,128)} %fusion.4, f32[192]{0:T(256)S(1)} %multiply_divide_fusion, bf16[192,4096]{1,0:T(8,128)(2,1)} %all-gather.7.cloned.1.call-done, ...), kind=kOutput, calls=%fused_computation.16 | convolution fusion | flops 6448742400 | bytes 47712512 | tf_op jit(solution)/shard_map/dot_general | solution.py:80
  363.5 2.4 fusion.16
  366.4 1.0 fusion.15
  367.4 1.5 collective-permute-start.17
  368.9 66.1 %psum.15 = f32[192]{0:T(256)S(1)} all-reduce(f32[192]{0:T(256)S(1)} %add.306), channel_id=1, replica_groups=mesh['row'=4,'col'=8] {'row','col'}, use_global_device_ids=true, to_apply=%region_7.8 | all-reduce | flops 192 | bytes 1536 | tf_op jit(solution)/shard_map/psum | solution.py:93
  435.0 3.4 fusion.12
  438.4 6.3 %fusion.9 = f32[8192,128]{1,0:T(8,128)} fusion(f32[8192,128]{1,0:T(8,128)S(1)} %fusion.12, bf16[192,8192]{1,0:T(8,128)(2,1)} %constant_dynamic-update-slice_fusion, f32[192]{0:T(256)S(1)} %bitcast.142, bf16[8192,4096]{1,0:T(8,128)(2,1)} %param.5, bf16[192,4096]{1,0:T(8,128)(2,1)} %all-gather.5.cloned.1.call-done), kind=kOutput, calls=%fused_computation.10 | convolution fusion | flops 411566080 | bytes 13681408 | tf_op jit(solution)/shard_map/dot_general | solution.py:114
  444.8 1.4 fusion.46
  446.3 1.6 collective-permute-start.24
  449.3 1.4 fusion.45
  450.8 3.2 collective-permute-start.20
  454.4 8.9 %collective-permute-start.18 = (f16[24,4096]{1,0:T(8,128)(2,1)S(1)}, f16[24,4096]{1,0:T(8,128)(2,1)S(1)}, u32[]{:S(2)}, u32[]{:S(2)}) collective-permute-start(f16[24,4096]{1,0:T(8,128)(2,1)S(1)} %get-tuple-element.26), channel_id=1, source_target_pairs={{0,2},{1,3},{2,4},{3,5},{4,6},{5,7},{6,0},{7,1},{8,10},{9,11},{10,... | collective-permute-start | bytes 589832 | tf_op jit(solution)/shard_map/ppermute | solution.py:43
  463.3 12.2 %collective-permute-done.23 = f16[24,4096]{1,0:T(8,128)(2,1)S(1)} collective-permute-done((f16[24,4096]{1,0:T(8,128)(2,1)S(1)}, f16[24,4096]{1,0:T(8,128)(2,1)S(1)}, u32[]{:S(2)}, u32[]{:S(2)}) %collective-permute-start.23) | collective-permute-done | bytes 196640 | tf_op jit(solution)/shard_map/ppermute | solution.py:43
  475.6 6.3 %collective-permute-done.19 = f16[24,4096]{1,0:T(8,128)(2,1)S(1)} collective-permute-done((f16[24,4096]{1,0:T(8,128)(2,1)S(1)}, f16[24,4096]{1,0:T(8,128)(2,1)S(1)}, u32[]{:S(2)}, u32[]{:S(2)}) %collective-permute-start.19) | collective-permute-done | bytes 196640 | tf_op jit(solution)/shard_map/ppermute | solution.py:43
  482.2 1.3 pad_maximum_fusion
  (78 shorter events, 15.3 us)
Async XLA Ops:
  7.2 8.9 %copy-start = (bf16[96,4096]{1,0:T(8,128)(2,1)S(1)}, bf16[96,4096]{1,0:T(8,128)(2,1)}, u32[]{:S(2)}) copy-start(bf16[96,4096]{1,0:T(8,128)(2,1)} %param.6) | copy-start | bytes 2359300
  7.2 71.0 %all-gather.5.cloned.1.call-start = ((), (), s32[]{:S(2)}) async-start(), calls=%async_computation | async-start | bytes 1966080 | tf_op jit(solution)/shard_map/all_gather | solution.py:72
  9.2 11.2 %copy-start.5 = (bf16[2,24,8192]{2,1,0:T(8,128)(2,1)S(1)}, bf16[2,24,8192]{2,1,0:T(8,128)(2,1)}, u32[]{:S(2)}) copy-start(bf16[2,24,8192]{2,1,0:T(8,128)(2,1)} %param.8) | copy-start | bytes 2359300
  9.3 19.7 %collective-permute-start.8 = (bf16[24,8192]{1,0:T(8,128)(2,1)S(1)}, bf16[24,8192]{1,0:T(8,128)(2,1)S(1)}, u32[]{:S(2)}, u32[]{:S(2)}) collective-permute-start(bf16[24,8192]{1,0:T(8,128)(2,1)S(1)} %get-tuple-element.25), channel_id=1, source_target_pairs={{0,1},{1,2},{2,3},{3,4},{4,5},{5,6},{6,7},{7,0},{8,9},{9,10},{10,1... | collective-permute-start | bytes 1179656 | tf_op jit(solution)/shard_map/ppermute | solution.py:20
  12.2 19.3 %collective-permute-start.9 = (bf16[24,8192]{1,0:T(8,128)(2,1)S(1)}, bf16[24,8192]{1,0:T(8,128)(2,1)S(1)}, u32[]{:S(2)}, u32[]{:S(2)}) collective-permute-start(bf16[24,8192]{1,0:T(8,128)(2,1)S(1)} %get-tuple-element.25), channel_id=1, source_target_pairs={{0,7},{1,0},{2,1},{3,2},{4,3},{5,4},{6,5},{7,6},{8,15},{9,8},{10,9... | collective-permute-start | bytes 1179656 | tf_op jit(solution)/shard_map/ppermute | solution.py:23
  18.3 263.1 %all-gather.7.cloned.1.call-start = ((), (), s32[]{:S(2)}) async-start(), calls=%async_computation.1 | async-start | bytes 1966080 | tf_op jit(solution)/shard_map/all_gather | solution.py:72
  29.0 18.5 %collective-permute-start.10 = (bf16[24,8192]{1,0:T(8,128)(2,1)S(1)}, bf16[24,8192]{1,0:T(8,128)(2,1)S(1)}, u32[]{:S(2)}, u32[]{:S(2)}) collective-permute-start(bf16[24,8192]{1,0:T(8,128)(2,1)S(1)} %collective-permute-done.8), channel_id=1, source_target_pairs={{0,1},{1,2},{2,3},{3,4},{4,5},{5,6},{6,7},{7,0},{8,9},{9,10},{10,1... | collective-permute-start | bytes 1179656 | tf_op jit(solution)/shard_map/ppermute | solution.py:20
  31.5 18.5 %collective-permute-start.11 = (bf16[24,8192]{1,0:T(8,128)(2,1)S(1)}, bf16[24,8192]{1,0:T(8,128)(2,1)S(1)}, u32[]{:S(2)}, u32[]{:S(2)}) collective-permute-start(bf16[24,8192]{1,0:T(8,128)(2,1)S(1)} %collective-permute-done.9), channel_id=1, source_target_pairs={{0,7},{1,0},{2,1},{3,2},{4,3},{5,4},{6,5},{7,6},{8,15},{9,8},{10,9... | collective-permute-start | bytes 1179656 | tf_op jit(solution)/shard_map/ppermute | solution.py:23
  47.5 17.6 %collective-permute-start.12 = (bf16[24,8192]{1,0:T(8,128)(2,1)S(1)}, bf16[24,8192]{1,0:T(8,128)(2,1)S(1)}, u32[]{:S(2)}, u32[]{:S(2)}) collective-permute-start(bf16[24,8192]{1,0:T(8,128)(2,1)S(1)} %collective-permute-done.10), channel_id=1, source_target_pairs={{0,1},{1,2},{2,3},{3,4},{4,5},{5,6},{6,7},{7,0},{8,9},{9,10},{10,1... | collective-permute-start | bytes 1179656 | tf_op jit(solution)/shard_map/ppermute | solution.py:20
  50.0 18.4 %collective-permute-start.13 = (bf16[24,8192]{1,0:T(8,128)(2,1)S(1)}, bf16[24,8192]{1,0:T(8,128)(2,1)S(1)}, u32[]{:S(2)}, u32[]{:S(2)}) collective-permute-start(bf16[24,8192]{1,0:T(8,128)(2,1)S(1)} %collective-permute-done.11), channel_id=1, source_target_pairs={{0,7},{1,0},{2,1},{3,2},{4,3},{5,4},{6,5},{7,6},{8,15},{9,8},{10,9... | collective-permute-start | bytes 1179656 | tf_op jit(solution)/shard_map/ppermute | solution.py:23
  65.1 12.2 %collective-permute-start.14 = (bf16[24,8192]{1,0:T(8,128)(2,1)S(1)}, bf16[24,8192]{1,0:T(8,128)(2,1)S(1)}, u32[]{:S(2)}, u32[]{:S(2)}) collective-permute-start(bf16[24,8192]{1,0:T(8,128)(2,1)S(1)} %collective-permute-done.12), channel_id=1, source_target_pairs={{0,1},{1,2},{2,3},{3,4},{4,5},{5,6},{6,7},{7,0},{8,9},{9,10},{10,1... | collective-permute-start | bytes 1179656 | tf_op jit(solution)/shard_map/ppermute | solution.py:20
  78.2 18.3 %copy-start.6 = (bf16[192,4096]{1,0:T(8,128)(2,1)S(1)}, bf16[192,4096]{1,0:T(8,128)(2,1)}, u32[]{:S(2)}) copy-start(bf16[192,4096]{1,0:T(8,128)(2,1)} %all-gather.5.cloned.1.call-done) | copy-start | bytes 4718596
  119.0 66.3 %collective-permute-start.4 = (f16[4,24,4096]{2,1,0:T(8,128)(2,1)}, f16[4,24,4096]{2,1,0:T(8,128)(2,1)S(1)}, u32[]{:S(2)}, u32[]{:S(2)}) collective-permute-start(f16[4,24,4096]{2,1,0:T(8,128)(2,1)} %fusion.14), channel_id=1, source_target_pairs={{0,1},{1,0},{2,3},{3,2},{4,5},{5,4},{6,7},{7,6},{8,9},{9,8},{10,11... | collective-permute-start | bytes 2359304 | tf_op jit(solution)/shard_map/ppermute | solution.py:36
  120.5 69.9 %collective-permute-start = (f16[4,24,4096]{2,1,0:T(8,128)(2,1)S(1)}, f16[4,24,4096]{2,1,0:T(8,128)(2,1)S(1)}, u32[]{:S(2)}, u32[]{:S(2)}) collective-permute-start(f16[4,24,4096]{2,1,0:T(8,128)(2,1)S(1)} %fusion.13), channel_id=1, source_target_pairs={{0,1},{1,0},{2,3},{3,2},{4,5},{5,4},{6,7},{7,6},{8,9},{9,8},{10,11... | collective-permute-start | bytes 2359304 | tf_op jit(solution)/shard_map/ppermute | solution.py:36
  185.2 5.2 %copy-start.2 = (f32[192,4096]{1,0:T(8,128)S(1)}, f32[192,4096]{1,0:T(8,128)}, u32[]{:S(2)}) copy-start(f32[192,4096]{1,0:T(8,128)} %get-tuple-element.18) | copy-start | bytes 9437188
  187.2 7.9 %collective-permute-start.7 = (f16[24,4096]{1,0:T(8,128)(2,1)S(1)}, f16[24,4096]{1,0:T(8,128)(2,1)S(1)}, u32[]{:S(2)}, u32[]{:S(2)}) collective-permute-start(f16[24,4096]{1,0:T(8,128)(2,1)S(1)} %get-tuple-element.38), channel_id=1, source_target_pairs={{0,6},{1,7},{2,0},{3,1},{4,2},{5,3},{6,4},{7,5},{8,14},{9,15},{10,... | collective-permute-start | bytes 589832 | tf_op jit(solution)/shard_map/ppermute | solution.py:43
  189.0 27.6 %collective-permute-start.6 = (f16[24,4096]{1,0:T(8,128)(2,1)S(1)}, f16[24,4096]{1,0:T(8,128)(2,1)S(1)}, u32[]{:S(2)}, u32[]{:S(2)}) collective-permute-start(f16[24,4096]{1,0:T(8,128)(2,1)S(1)} %get-tuple-element.39), channel_id=1, source_target_pairs={{0,4},{1,5},{2,6},{3,7},{4,0},{5,1},{6,2},{7,3},{8,12},{9,13},{10,... | collective-permute-start | bytes 589832 | tf_op jit(solution)/shard_map/ppermute | solution.py:43
  189.7 26.9 %collective-permute-start.5 = (f16[24,4096]{1,0:T(8,128)(2,1)S(1)}, f16[24,4096]{1,0:T(8,128)(2,1)S(1)}, u32[]{:S(2)}, u32[]{:S(2)}) collective-permute-start(f16[24,4096]{1,0:T(8,128)(2,1)S(1)} %get-tuple-element.37), channel_id=1, source_target_pairs={{0,2},{1,3},{2,4},{3,5},{4,6},{5,7},{6,0},{7,1},{8,10},{9,11},{10,... | collective-permute-start | bytes 589832 | tf_op jit(solution)/shard_map/ppermute | solution.py:43
  190.8 25.9 %collective-permute-start.3 = (f16[24,4096]{1,0:T(8,128)(2,1)S(1)}, f16[24,4096]{1,0:T(8,128)(2,1)S(1)}, u32[]{:S(2)}, u32[]{:S(2)}) collective-permute-start(f16[24,4096]{1,0:T(8,128)(2,1)S(1)} %get-tuple-element.35), channel_id=1, source_target_pairs={{0,6},{1,7},{2,0},{3,1},{4,2},{5,3},{6,4},{7,5},{8,14},{9,15},{10,... | collective-permute-start | bytes 589832 | tf_op jit(solution)/shard_map/ppermute | solution.py:43
  194.0 29.0 %collective-permute-start.2 = (f16[24,4096]{1,0:T(8,128)(2,1)S(1)}, f16[24,4096]{1,0:T(8,128)(2,1)S(1)}, u32[]{:S(2)}, u32[]{:S(2)}) collective-permute-start(f16[24,4096]{1,0:T(8,128)(2,1)S(1)} %get-tuple-element.36), channel_id=1, source_target_pairs={{0,4},{1,5},{2,6},{3,7},{4,0},{5,1},{6,2},{7,3},{8,12},{9,13},{10,... | collective-permute-start | bytes 589832 | tf_op jit(solution)/shard_map/ppermute | solution.py:43
  195.1 27.9 %collective-permute-start.1 = (f16[24,4096]{1,0:T(8,128)(2,1)S(1)}, f16[24,4096]{1,0:T(8,128)(2,1)S(1)}, u32[]{:S(2)}, u32[]{:S(2)}) collective-permute-start(f16[24,4096]{1,0:T(8,128)(2,1)S(1)} %get-tuple-element.34), channel_id=1, source_target_pairs={{0,2},{1,3},{2,4},{3,5},{4,6},{5,7},{6,0},{7,1},{8,10},{9,11},{10,... | collective-permute-start | bytes 589832 | tf_op jit(solution)/shard_map/ppermute | solution.py:43
  223.3 2.2 collective-permute-start.15
  224.0 7.8 %collective-permute-start.16 = (f32[24,4096]{1,0:T(8,128)S(1)}, f32[24,4096]{1,0:T(8,128)S(1)}, u32[]{:S(2)}, u32[]{:S(2)}) collective-permute-start(f32[24,4096]{1,0:T(8,128)S(1)} %get-tuple-element.32), channel_id=1, source_target_pairs={{0,1},{1,0},{2,9},{3,8},{4,17},{5,16},{6,25},{7,24},{8,3},{9,2},{1... | collective-permute-start | bytes 1179656 | tf_op jit(solution)/shard_map/ppermute | solution.py:108
  233.1 110.9 %all-gather.9.cloned.1.call-start = ((), (), s32[]{:S(2)}) async-start(), calls=%async_computation.2 | async-start | bytes 3538944 | tf_op jit(solution)/shard_map/all_gather | solution.py:77
  365.8 78.9 %collective-permute-start.21 = (f16[4,24,4096]{2,1,0:T(8,128)(2,1)}, f16[4,24,4096]{2,1,0:T(8,128)(2,1)}, u32[]{:S(2)}, u32[]{:S(2)}) collective-permute-start(f16[4,24,4096]{2,1,0:T(8,128)(2,1)} %fusion.16), channel_id=1, source_target_pairs={{0,1},{1,0},{2,3},{3,2},{4,5},{5,4},{6,7},{7,6},{8,9},{9,8},{10,11... | collective-permute-start | bytes 2359304 | tf_op jit(solution)/shard_map/ppermute | solution.py:36
  367.4 81.9 %collective-permute-start.17 = (f16[4,24,4096]{2,1,0:T(8,128)(2,1)}, f16[4,24,4096]{2,1,0:T(8,128)(2,1)}, u32[]{:S(2)}, u32[]{:S(2)}) collective-permute-start(f16[4,24,4096]{2,1,0:T(8,128)(2,1)} %fusion.15), channel_id=1, source_target_pairs={{0,1},{1,0},{2,3},{3,2},{4,5},{5,4},{6,7},{7,6},{8,9},{9,8},{10,11... | collective-permute-start | bytes 2359304 | tf_op jit(solution)/shard_map/ppermute | solution.py:36
  438.4 6.3 %copy-start.3 = (f32[192,4096]{1,0:T(8,128)S(1)}, f32[192,4096]{1,0:T(8,128)}, u32[]{:S(2)}) copy-start(f32[192,4096]{1,0:T(8,128)} %get-tuple-element.17) | copy-start | bytes 9437188
  446.3 8.1 %collective-permute-start.24 = (f16[24,4096]{1,0:T(8,128)(2,1)S(1)}, f16[24,4096]{1,0:T(8,128)(2,1)S(1)}, u32[]{:S(2)}, u32[]{:S(2)}) collective-permute-start(f16[24,4096]{1,0:T(8,128)(2,1)S(1)} %get-tuple-element.30), channel_id=1, source_target_pairs={{0,6},{1,7},{2,0},{3,1},{4,2},{5,3},{6,4},{7,5},{8,14},{9,15},{10,... | collective-permute-start | bytes 589832 | tf_op jit(solution)/shard_map/ppermute | solution.py:43
  447.9 27.7 %collective-permute-start.23 = (f16[24,4096]{1,0:T(8,128)(2,1)S(1)}, f16[24,4096]{1,0:T(8,128)(2,1)S(1)}, u32[]{:S(2)}, u32[]{:S(2)}) collective-permute-start(f16[24,4096]{1,0:T(8,128)(2,1)S(1)} %get-tuple-element.31), channel_id=1, source_target_pairs={{0,4},{1,5},{2,6},{3,7},{4,0},{5,1},{6,2},{7,3},{8,12},{9,13},{10,... | collective-permute-start | bytes 589832 | tf_op jit(solution)/shard_map/ppermute | solution.py:43
  448.6 26.9 %collective-permute-start.22 = (f16[24,4096]{1,0:T(8,128)(2,1)S(1)}, f16[24,4096]{1,0:T(8,128)(2,1)S(1)}, u32[]{:S(2)}, u32[]{:S(2)}) collective-permute-start(f16[24,4096]{1,0:T(8,128)(2,1)S(1)} %get-tuple-element.29), channel_id=1, source_target_pairs={{0,2},{1,3},{2,4},{3,5},{4,6},{5,7},{6,0},{7,1},{8,10},{9,11},{10,... | collective-permute-start | bytes 589832 | tf_op jit(solution)/shard_map/ppermute | solution.py:43
  450.7 31.5 %copy-start.4 = (f32[1,24,8192]{2,1,0:T(8,128)S(1)}, f32[1,24,8192]{2,1,0:T(8,128)}, u32[]{:S(2)}) copy-start(f32[1,24,8192]{2,1,0:T(8,128)} %maximum_divide_fusion.2) | copy-start | bytes 2359300
  450.8 24.8 %collective-permute-start.20 = (f16[24,4096]{1,0:T(8,128)(2,1)S(1)}, f16[24,4096]{1,0:T(8,128)(2,1)S(1)}, u32[]{:S(2)}, u32[]{:S(2)}) collective-permute-start(f16[24,4096]{1,0:T(8,128)(2,1)S(1)} %get-tuple-element.27), channel_id=1, source_target_pairs={{0,6},{1,7},{2,0},{3,1},{4,2},{5,3},{6,4},{7,5},{8,14},{9,15},{10,... | collective-permute-start | bytes 589832 | tf_op jit(solution)/shard_map/ppermute | solution.py:43
  454.0 27.9 %collective-permute-start.19 = (f16[24,4096]{1,0:T(8,128)(2,1)S(1)}, f16[24,4096]{1,0:T(8,128)(2,1)S(1)}, u32[]{:S(2)}, u32[]{:S(2)}) collective-permute-start(f16[24,4096]{1,0:T(8,128)(2,1)S(1)} %get-tuple-element.28), channel_id=1, source_target_pairs={{0,4},{1,5},{2,6},{3,7},{4,0},{5,1},{6,2},{7,3},{8,12},{9,13},{10,... | collective-permute-start | bytes 589832 | tf_op jit(solution)/shard_map/ppermute | solution.py:43
  454.4 27.6 %collective-permute-start.18 = (f16[24,4096]{1,0:T(8,128)(2,1)S(1)}, f16[24,4096]{1,0:T(8,128)(2,1)S(1)}, u32[]{:S(2)}, u32[]{:S(2)}) collective-permute-start(f16[24,4096]{1,0:T(8,128)(2,1)S(1)} %get-tuple-element.26), channel_id=1, source_target_pairs={{0,2},{1,3},{2,4},{3,5},{4,6},{5,7},{6,0},{7,1},{8,10},{9,11},{10,... | collective-permute-start | bytes 589832 | tf_op jit(solution)/shard_map/ppermute | solution.py:43
  475.5 7.9 %copy-start.1 = (bf16[96,4096]{1,0:T(8,128)(2,1)S(1)}, bf16[96,4096]{1,0:T(8,128)(2,1)}, u32[]{:S(2)}) copy-start(bf16[96,4096]{1,0:T(8,128)(2,1)} %param.6) | copy-start | bytes 2359300
Sparse Core Ops, SparseCore 0:
  18.4 18.3 all-gather.4
  233.2 48.0 all-gather.6
  283.6 60.4 all-gather.8
